TPU v7x, 128 devices: a whole 4x4x4 slice. The times are simulated.
128 devices in a mesh: row: 16 (over x, z), col: 8 (over y, core).
Axes of the slice: x: 4, y: 4, z: 4, core: 2. Of those that a mesh axis runs over, the one named last changes fastest.
Arguments:
- phi_modes: bfloat16 [1536, 1024, 512], P(('row', 'col')), may hold values from -6 to 6
- trace_maps: bfloat16 [1536, 256, 1024], P(('row', 'col')), may hold values from -0.1875 to 0.1875
- mortar: bfloat16 [1024, 256, 256], P(('row', 'col')), may hold values from -0.0234375 to 0.0234375
- pair_list: int32 [1024, 2], P(('row', 'col')), may hold values from 0 to 1535, as said below
- iface_counts: int32 [1024], P(('row', 'col')), may hold values from 64 to 256
Outputs:
- coupling: bfloat16 [1024, 512, 512], P(('row', 'col'))
Inputs may be any that keep to these rules, and one draw needn't show every extreme that they name: Substructure s belongs to device s // 12, devices numbered row-major over (row, col). Row p of pair_list lies on the device that owns its i; its j is owned by that device or by a neighbouring device one step along row (no wrap) or along col (cyclic). Of one device's 8 pairs at most 2 have j on any one other device, and that many do in every draw; every existing neighbouring device owns the j of some pair of the device.
All inputs are finite; a program needn't handle non-finite values.
Results may differ from a plain program's by a relative error of at most 0.0064.
Values may be sent and summed in bfloat16 or wider, within the bound.
A program may use at most 128 MiB of HBM per device.

v0:
```python
import jax
import jax.numpy as jnp
from jax import lax
from jax.sharding import PartitionSpec as P


def extended(block, sides, width, periodic):
    for axis, dim in sides:
        count = lax.axis_size(axis)
        forward = [(i, i + 1) for i in range(count - 1)]
        if periodic:
            forward.append((count - 1, 0))
        backward = [(target, source) for source, target in forward]
        low = lax.ppermute(
            lax.slice_in_dim(block, block.shape[dim] - width, None, axis=dim), axis, forward
        )
        high = lax.ppermute(lax.slice_in_dim(block, 0, width, axis=dim), axis, backward)
        block = jnp.concatenate([low, block, high], axis=dim)
    return block


def body(phi_modes, trace_maps, mortar, pair_list, iface_counts):
    owned = phi_modes.shape[0]
    iface = mortar.shape[1]
    ncol = lax.axis_size("col")
    my_row = lax.axis_index("row")
    my_col = lax.axis_index("col")
    my_dev = my_row * ncol + my_col
    panels = jnp.einsum(
        "snb,sbk->snk", trace_maps, phi_modes, preferred_element_type=jnp.float32
    ).astype(jnp.bfloat16)
    first = pair_list[:, 0]
    second = pair_list[:, 1]
    local_first = first - my_dev * owned
    owner = second // owned
    owner_row = owner // ncol
    owner_col = owner % ncol
    within = second % owned
    code = jnp.where(
        owner == my_dev,
        0,
        jnp.where(
            owner_row == my_row - 1,
            1,
            jnp.where(
                owner_row == my_row + 1, 2, jnp.where(owner_col == (my_col - 1) % ncol, 3, 4)
            ),
        ),
    )
    row_table = extended(panels, (("row", 0),), owned, False)
    col_table = extended(panels, (("col", 0),), owned, True)
    table = jnp.concatenate([row_table, col_table[:owned], col_table[2 * owned :]], 0)
    starts = jnp.array([1, 0, 2, 3, 4], jnp.int32) * owned
    position = starts[code] + within
    partner = table[position]
    own_panel = panels[local_first]
    inside = jnp.arange(iface, dtype=jnp.int32)[None, :] < iface_counts[:, None]
    keep = (inside[:, :, None] & inside[:, None, :]).astype(jnp.bfloat16)
    masked = mortar * keep
    applied = jnp.einsum(
        "pnm,pmk->pnk", masked, partner, preferred_element_type=jnp.float32
    ).astype(jnp.bfloat16)
    coupling = jnp.einsum("pnk,pnl->pkl", own_panel, applied, preferred_element_type=jnp.float32)
    return coupling.astype(jnp.bfloat16)


def solution(mesh):
    return jax.shard_map(
        body,
        mesh=mesh,
        in_specs=(
            P(("row", "col"), None, None),
            P(("row", "col"), None, None),
            P(("row", "col"), None, None),
            P(("row", "col"), None),
            P(("row", "col")),
        ),
        out_specs=P(("row", "col"), None, None),
        check_vma=False,
    )
```

profile of v0, /device:TPU:22, one launch (start us, length us, event | category | flops | bytes accessed | tf_op | source)
XLA Modules:
  0.0 114.2 jit_solution(11228578858839102943)
XLA Ops:
  0.0 0.0 copy-start
  0.0 0.0 copy-start.2
  0.0 9.8 %convolution_convert_fusion.1 = bf16[12,256,512]{2,1,0:T(8,128)(2,1)S(1)} fusion(bf16[12,256,1024]{2,1,0:T(8,128)(2,1)} %param.7, bf16[12,1024,512]{2,1,0:T(8,128)(2,1)} %param.6), kind=kOutput, calls=%fused_computation.4 | convolution fusion | flops 3222798336 | bytes 22020096 | tf_op jit(solution)/shard_map/snb,sbk->snk/dot_general | solution.py:29
  9.8 0.0 copy-start.3
  9.9 3.8 %collective-permute-start = (bf16[12,256,512]{2,1,0:T(8,128)(2,1)S(1)}, bf16[12,256,512]{2,1,0:T(8,128)(2,1)}, u32[]{:S(2)}, u32[]{:S(2)}) collective-permute-start(bf16[12,256,512]{2,1,0:T(8,128)(2,1)S(1)} %convolution_convert_fusion.1), channel_id=1, source_target_pairs={{0,8},{8,16},{16,24},{24,32},{32,40},{40,48},{48,56},{56,64},{64,7... | collective-permute-start | bytes 9437192 | tf_op jit(solution)/shard_map/ppermute | solution.py:14
  13.7 4.3 %collective-permute-start.1 = (bf16[12,256,512]{2,1,0:T(8,128)(2,1)S(1)}, bf16[12,256,512]{2,1,0:T(8,128)(2,1)}, u32[]{:S(2)}, u32[]{:S(2)}) collective-permute-start(bf16[12,256,512]{2,1,0:T(8,128)(2,1)S(1)} %convolution_convert_fusion.1), channel_id=1, source_target_pairs={{8,0},{16,8},{24,16},{32,24},{40,32},{48,40},{56,48},{64,56},{72,6... | collective-permute-start | bytes 9437192 | tf_op jit(solution)/shard_map/ppermute | solution.py:17
  18.0 0.0 collective-permute-start.2
  18.0 1.7 %collective-permute-start.3 = (bf16[12,256,512]{2,1,0:T(8,128)(2,1)S(1)}, bf16[12,256,512]{2,1,0:T(8,128)(2,1)}, u32[]{:S(2)}, u32[]{:S(2)}) collective-permute-start(bf16[12,256,512]{2,1,0:T(8,128)(2,1)S(1)} %convolution_convert_fusion.1), channel_id=1, source_target_pairs={{1,0},{2,1},{3,2},{4,3},{5,4},{6,5},{7,6},{0,7},{9,8},{10,9},{11,1... | collective-permute-start | bytes 9437192 | tf_op jit(solution)/shard_map/ppermute | solution.py:17
  19.8 0.0 copy-done.2
  19.8 0.0 copy-done
  19.8 0.6 gather_fusion.1
  20.5 2.0 %gather_fusion = bf16[8,256,512]{2,1,0:T(8,128)(2,1)} fusion(bf16[12,256,512]{2,1,0:T(8,128)(2,1)S(1)} %convolution_convert_fusion.1, s32[1024]{0:T(1024)S(1)} %get-tuple-element.8), kind=kCustom, calls=%fused_computation | custom fusion | bytes 4194336 | tf_op jit(solution)/shard_map/gather | solution.py:56
  22.5 0.0 copy-done.3
  22.5 0.1 iota_compare_fusion
  22.6 61.7 %collective-permute-done = bf16[12,256,512]{2,1,0:T(8,128)(2,1)} collective-permute-done((bf16[12,256,512]{2,1,0:T(8,128)(2,1)S(1)}, bf16[12,256,512]{2,1,0:T(8,128)(2,1)}, u32[]{:S(2)}, u32[]{:S(2)}) %collective-permute-start) | collective-permute-done | bytes 3145760 | tf_op jit(solution)/shard_map/ppermute | solution.py:14
  84.3 3.7 %constant_dynamic-update-slice_fusion.4 = bf16[60,256,512]{2,1,0:T(8,128)(2,1)} fusion(bf16[12,256,512]{2,1,0:T(8,128)(2,1)} %collective-permute-done), kind=kLoop, calls=%fused_computation.15 | loop fusion | bytes 6291456
  88.0 1.9 %constant_dynamic-update-slice_fusion.3 = bf16[60,256,512]{2,1,0:T(8,128)(2,1)} fusion(bf16[60,256,512]{2,1,0:T(8,128)(2,1)} %constant_dynamic-update-slice_fusion.4, bf16[12,256,512]{2,1,0:T(8,128)(2,1)S(1)} %convolution_convert_fusion.1), kind=kLoop, calls=%fused_computation.14 | loop fusion | bytes 6291456
  89.9 0.0 collective-permute-done.1
  89.9 3.8 %constant_dynamic-update-slice_fusion.2 = bf16[60,256,512]{2,1,0:T(8,128)(2,1)} fusion(bf16[60,256,512]{2,1,0:T(8,128)(2,1)} %constant_dynamic-update-slice_fusion.3, bf16[12,256,512]{2,1,0:T(8,128)(2,1)} %collective-permute-done.1), kind=kLoop, calls=%fused_computation.13 | loop fusion | bytes 6291456
  93.7 0.0 collective-permute-done.2
  93.7 3.7 %constant_dynamic-update-slice_fusion.1 = bf16[60,256,512]{2,1,0:T(8,128)(2,1)} fusion(bf16[60,256,512]{2,1,0:T(8,128)(2,1)} %constant_dynamic-update-slice_fusion.2, bf16[12,256,512]{2,1,0:T(8,128)(2,1)} %collective-permute-done.2), kind=kLoop, calls=%fused_computation.12 | loop fusion | bytes 6291456
  97.4 0.0 collective-permute-done.3
  97.4 0.0 copy-start.1
  97.4 0.0 copy-start.4
  97.4 3.9 %constant_dynamic-update-slice_fusion = bf16[60,256,512]{2,1,0:T(8,128)(2,1)} fusion(bf16[60,256,512]{2,1,0:T(8,128)(2,1)} %constant_dynamic-update-slice_fusion.1, bf16[12,256,512]{2,1,0:T(8,128)(2,1)} %collective-permute-done.3), kind=kLoop, calls=%fused_computation.11 | loop fusion | bytes 6291456 | tf_op jit(solution)/shard_map/concatenate | solution.py:52
  101.3 7.5 %gather_fusion.2 = bf16[8,256,512]{2,1,0:T(8,128)(2,1)} fusion(bf16[60,256,512]{2,1,0:T(8,128)(2,1)} %constant_dynamic-update-slice_fusion, s32[1024]{0:T(1024)S(1)} %get-tuple-element.7), kind=kCustom, calls=%fused_computation.2 | custom fusion | bytes 4194336 | tf_op jit(solution)/shard_map/gather | solution.py:55
  108.8 0.0 copy-done.1
  108.8 0.0 copy-done.4
  108.8 5.5 %convolution_convert_fusion = bf16[8,512,512]{2,1,0:T(8,128)(2,1)} fusion(bf16[8,256,512]{2,1,0:T(8,128)(2,1)S(1)} %copy-done.1, bf16[8,256,512]{2,1,0:T(8,128)(2,1)} %gather_fusion.2, bf16[8,256,256]{2,1,0:T(8,128)(2,1)S(1)} %copy-done.4, pred[8,256]{1,0:T(8,128)(4,1)S(1)} %iota_compare_fusion), kind=kOutput, calls=%fused_computation.3 | convolution fusion | flops 1614807040 | bytes 9439232 | tf_op jit(solution)/shard_map/pnk,pnl->pkl/dot_general | solution.py:63
  (4 shorter events, 0.1 us)
Async XLA Ops:
  0.0 19.8 %copy-start = (s32[5]{0:T(128)S(1)}, s32[5]{0:T(128)}, u32[]{:S(2)}) copy-start(s32[5]{0:T(128)} %constant.81) | copy-start | bytes 64
  0.0 19.8 %copy-start.2 = (s32[8,2]{0,1:T(2,128)S(1)}, s32[8,2]{0,1:T(2,128)}, u32[]{:S(2)}) copy-start(s32[8,2]{0,1:T(2,128)} %param.9) | copy-start | bytes 196
  9.8 12.7 %copy-start.3 = (s32[8]{0:T(128)S(1)}, s32[8]{0:T(128)}, u32[]{:S(2)}) copy-start(s32[8]{0:T(128)} %param.10) | copy-start | bytes 100
  9.9 74.4 %collective-permute-start = (bf16[12,256,512]{2,1,0:T(8,128)(2,1)S(1)}, bf16[12,256,512]{2,1,0:T(8,128)(2,1)}, u32[]{:S(2)}, u32[]{:S(2)}) collective-permute-start(bf16[12,256,512]{2,1,0:T(8,128)(2,1)S(1)} %convolution_convert_fusion.1), channel_id=1, source_target_pairs={{0,8},{8,16},{16,24},{24,32},{32,40},{40,48},{48,56},{56,64},{64,7... | collective-permute-start | bytes 9437192 | tf_op jit(solution)/shard_map/ppermute | solution.py:14
  13.7 76.2 %collective-permute-start.1 = (bf16[12,256,512]{2,1,0:T(8,128)(2,1)S(1)}, bf16[12,256,512]{2,1,0:T(8,128)(2,1)}, u32[]{:S(2)}, u32[]{:S(2)}) collective-permute-start(bf16[12,256,512]{2,1,0:T(8,128)(2,1)S(1)} %convolution_convert_fusion.1), channel_id=1, source_target_pairs={{8,0},{16,8},{24,16},{32,24},{40,32},{48,40},{56,48},{64,56},{72,6... | collective-permute-start | bytes 9437192 | tf_op jit(solution)/shard_map/ppermute | solution.py:17
  18.0 75.7 %collective-permute-start.2 = (bf16[12,256,512]{2,1,0:T(8,128)(2,1)S(1)}, bf16[12,256,512]{2,1,0:T(8,128)(2,1)}, u32[]{:S(2)}, u32[]{:S(2)}) collective-permute-start(bf16[12,256,512]{2,1,0:T(8,128)(2,1)S(1)} %convolution_convert_fusion.1), channel_id=1, source_target_pairs={{0,1},{1,2},{2,3},{3,4},{4,5},{5,6},{6,7},{7,0},{8,9},{9,10},{10,1... | collective-permute-start | bytes 9437192 | tf_op jit(solution)/shard_map/ppermute | solution.py:14
  18.0 79.4 %collective-permute-start.3 = (bf16[12,256,512]{2,1,0:T(8,128)(2,1)S(1)}, bf16[12,256,512]{2,1,0:T(8,128)(2,1)}, u32[]{:S(2)}, u32[]{:S(2)}) collective-permute-start(bf16[12,256,512]{2,1,0:T(8,128)(2,1)S(1)} %convolution_convert_fusion.1), channel_id=1, source_target_pairs={{1,0},{2,1},{3,2},{4,3},{5,4},{6,5},{7,6},{0,7},{9,8},{10,9},{11,1... | collective-permute-start | bytes 9437192 | tf_op jit(solution)/shard_map/ppermute | solution.py:17
  97.4 11.3 %copy-start.1 = (bf16[8,256,512]{2,1,0:T(8,128)(2,1)S(1)}, bf16[8,256,512]{2,1,0:T(8,128)(2,1)}, u32[]{:S(2)}) copy-start(bf16[8,256,512]{2,1,0:T(8,128)(2,1)} %gather_fusion) | copy-start | bytes 6291460
  97.4 11.3 %copy-start.4 = (bf16[8,256,256]{2,1,0:T(8,128)(2,1)S(1)}, bf16[8,256,256]{2,1,0:T(8,128)(2,1)}, u32[]{:S(2)}) copy-start(bf16[8,256,256]{2,1,0:T(8,128)(2,1)} %param.8) | copy-start | bytes 3145732
where the time goes:
time: 115 us; the launch traced here: 114 us
  waiting for transfers between devices  61.7 us (54%)
  local copies, waits for them, and re-layouts  27.2 us (24%)
  matrix products  15.3 us (13%)
  starting transfers between devices  9.88 us (9%)
    ppermute x2, waiting for transfers between devices, extended(): lax.ppermute(lax.slice_in_dim(block, block.shape[dim] - width, None, axis...  61.7 us
    unnamed x14, local copies, waits for them, and re-layouts  13.2 us
    dot_general x1, matrix products, body(): jnp.einsum('snb,sbk->snk', trace_maps, phi_modes, preferred_element_type=...  9.83 us
    gather x1, local copies, waits for them, and re-layouts, body(): partner = table[position]  7.45 us
    ppermute x2, starting transfers between devices, extended(): lax.ppermute(lax.slice_in_dim(block, 0, width, axis=dim), axis, backward)  6.04 us
    dot_general x1, matrix products, body(): jnp.einsum('pnk,pnl->pkl', own_panel, applied, preferred_element_type=jnp...  5.46 us
    concatenate x1, local copies, waits for them, and re-layouts, body(): jnp.concatenate([row_table, col_table[:owned], col_table[2 * owned:]], 0)  3.88 us
    ppermute x2, starting transfers between devices, extended(): lax.ppermute(lax.slice_in_dim(block, block.shape[dim] - width, None, axis...  3.85 us
  transfers between devices with their start and end apart: 4, of which 1 were waited for; matrix products, arithmetic and copies ran while one was open for 14% of the time, Pallas kernels for 0%

commit v1 on v0

v1 whole, which is shorter than its diff:
```python
import functools

import jax
import jax.numpy as jnp
from jax import lax
from jax.experimental import pallas as pl
from jax.experimental.pallas import tpu as pltpu
from jax.sharding import PartitionSpec as P

MESH = pl.DeviceIdType.MESH
WIDTH = 256
CAP = 2


def panels_kernel(
    nrow,
    ncol,
    phi_hbm,
    trace_hbm,
    mortar_hbm,
    pairs,
    counts,
    panels,
    arrived,
    left,
    route,
    phi,
    trace,
    mortar,
    outgoing,
    wanted,
    asked,
    phi_sem,
    trace_sem,
    mortar_sem,
    ask_send,
    ask_recv,
    send_sem,
    recv_sem,
):
    parts, owned, iface, width = panels.shape
    npair = mortar.shape[0]
    row = lax.axis_index("row")
    col = lax.axis_index("col")
    mine = row * ncol + col
    near = [
        (lax.rem(row + nrow - 1, nrow), col),
        (lax.rem(row + 1, nrow), col),
        (row, lax.rem(col + ncol - 1, ncol)),
        (row, lax.rem(col + 1, ncol)),
    ]

    barrier = pltpu.get_barrier_semaphore()
    for device in near:
        pl.semaphore_signal(barrier, inc=1, device_id=device, device_id_type=MESH)

    def trace_copy(s):
        return pltpu.make_async_copy(trace_hbm.at[s], trace.at[s], trace_sem.at[s])

    def phi_copy(c, s):
        return pltpu.make_async_copy(
            phi_hbm.at[s, :, pl.ds(c * width, width)], phi.at[c, s], phi_sem.at[c, s]
        )

    mortar_copy = pltpu.make_async_copy(mortar_hbm, mortar, mortar_sem)

    @pl.loop(0, owned)
    def _(s):
        trace_copy(s).start()
        phi_copy(0, s).start()

    for c in range(1, parts):
        @pl.loop(0, owned)
        def _(s):
            phi_copy(c, s).start()

    mortar_copy.start()

    base = [(r * ncol + k) * owned for r, k in near]
    taken = [jnp.int32(0)] * 4
    first = [jnp.int32(0)] * 4
    second = [jnp.int32(0)] * 4
    for p in range(npair):
        j = pairs[1, p]
        place = jnp.clip(j - mine * owned, 0, owned - 1)
        for d in range(4):
            local = j - base[d]
            hit = (local >= 0) & (local < owned)
            first[d] = jnp.where(hit & (taken[d] == 0), local, first[d])
            second[d] = jnp.where(hit & (taken[d] == 1), local, second[d])
            place = jnp.where(hit, owned + CAP * d + jnp.minimum(taken[d], CAP - 1), place)
            taken[d] = taken[d] + hit.astype(jnp.int32)
        route[p] = place
    for d in range(4):
        wanted[d, 0] = first[d]
        wanted[d, 1] = second[d]

    pl.semaphore_wait(barrier, 4)
    asks = [
        pltpu.make_async_remote_copy(
            src_ref=wanted.at[d],
            dst_ref=asked.at[d ^ 1],
            send_sem=ask_send.at[d],
            recv_sem=ask_recv.at[d ^ 1],
            device_id=near[d],
            device_id_type=MESH,
        )
        for d in range(4)
    ]
    for ask in asks:
        ask.start()

    sends = []
    for c in range(parts):
        @pl.loop(0, owned)
        def _(s):
            if c == 0:
                trace_copy(s).wait()
            phi_copy(c, s).wait()
            panels[c, s] = jnp.dot(
                trace[s], phi[c, s], preferred_element_type=jnp.float32
            ).astype(panels.dtype)

        if c == 0:
            for ask in asks:
                ask.wait()
        for d in range(4):
            for k in range(CAP):
                outgoing[c, d, k] = panels[c, asked[d, k]]
            send = pltpu.make_async_remote_copy(
                src_ref=outgoing.at[c, d],
                dst_ref=arrived.at[c, d ^ 1],
                send_sem=send_sem.at[c, d],
                recv_sem=recv_sem.at[c, d ^ 1],
                device_id=near[d],
                device_id_type=MESH,
            )
            send.start()
            sends.append(send)

    mortar_copy.wait()
    rows = lax.broadcasted_iota(jnp.int32, (iface, iface), 0)
    columns = lax.broadcasted_iota(jnp.int32, (iface, iface), 1)

    @pl.loop(0, npair)
    def _(p):
        own = jnp.clip(pairs[0, p] - mine * owned, 0, owned - 1)
        count = counts[p]
        keep = (rows < count) & (columns < count)
        masked = jnp.where(keep, mortar[p].astype(jnp.float32), 0.0).astype(mortar.dtype)
        for c in range(parts):
            left[p, pl.ds(c * width, width), :] = lax.dot_general(
                panels[c, own],
                masked,
                (((0,), (0,)), ((), ())),
                preferred_element_type=jnp.float32,
            ).astype(left.dtype)

    for send in sends:
        send.wait()


def coupling_kernel(route, panels, arrived, left, coupling):
    parts, owned, iface, width = panels.shape
    p = pl.program_id(0)
    place = route[p]

    def multiply(partner):
        for c in range(parts):
            coupling[0, :, pl.ds(c * width, width)] = jnp.dot(
                left[p], partner(c), preferred_element_type=jnp.float32
            ).astype(coupling.dtype)

    @pl.when(place < owned)
    def _():
        multiply(lambda c: panels[c, place])

    @pl.when(place >= owned)
    def _():
        multiply(lambda c: arrived[c, (place - owned) // CAP, (place - owned) % CAP])


def body(nrow, ncol, phi_modes, trace_maps, mortar, pair_list, iface_counts):
    owned, boundary, modes = phi_modes.shape
    npair, iface, _ = mortar.shape
    parts = modes // WIDTH
    dtype = phi_modes.dtype
    hbm = pl.BlockSpec(memory_space=pltpu.HBM)
    smem = pl.BlockSpec(memory_space=pltpu.SMEM)
    vmem = pl.BlockSpec(memory_space=pltpu.VMEM)
    dma = pltpu.SemaphoreType.DMA
    panels, arrived, left, route = pl.pallas_call(
        functools.partial(panels_kernel, nrow, ncol),
        out_shape=(
            pltpu.VMEM((parts, owned, iface, WIDTH), dtype),
            pltpu.VMEM((parts, 4, CAP, iface, WIDTH), dtype),
            pltpu.VMEM((npair, modes, iface), dtype),
            pltpu.SMEM((npair,), jnp.int32),
        ),
        in_specs=[hbm, hbm, hbm, smem, smem],
        out_specs=(vmem, vmem, vmem, smem),
        scratch_shapes=[
            pltpu.VMEM((parts, owned, boundary, WIDTH), dtype),
            pltpu.VMEM((owned, iface, boundary), dtype),
            pltpu.VMEM((npair, iface, iface), dtype),
            pltpu.VMEM((parts, 4, CAP, iface, WIDTH), dtype),
            pltpu.SMEM((4, 128), jnp.int32),
            pltpu.SMEM((4, 128), jnp.int32),
            dma((parts, owned)),
            dma((owned,)),
            dma,
            dma((4,)),
            dma((4,)),
            dma((parts, 4)),
            dma((parts, 4)),
        ],
        compiler_params=pltpu.CompilerParams(
            collective_id=0, has_side_effects=True, vmem_limit_bytes=48 * 2**20
        ),
        name="panels",
    )(phi_modes, trace_maps, mortar, pair_list.T, iface_counts)
    return pl.pallas_call(
        coupling_kernel,
        out_shape=jax.ShapeDtypeStruct((npair, modes, modes), dtype),
        grid=(npair,),
        in_specs=[smem, vmem, vmem, vmem],
        out_specs=pl.BlockSpec((1, modes, modes), lambda p: (p, 0, 0)),
        compiler_params=pltpu.CompilerParams(vmem_limit_bytes=32 * 2**20),
        name="coupling",
    )(route, panels, arrived, left)


def solution(mesh):
    return jax.shard_map(
        functools.partial(body, mesh.shape["row"], mesh.shape["col"]),
        mesh=mesh,
        in_specs=(
            P(("row", "col"), None, None),
            P(("row", "col"), None, None),
            P(("row", "col"), None, None),
            P(("row", "col"), None),
            P(("row", "col")),
        ),
        out_specs=P(("row", "col"), None, None),
        check_vma=False,
    )
```

time: 115 us -> 30 us (0.26)
  the two profiles are of different devices: /device:TPU:22 before, /device:TPU:0 now
where the time goes in v1:
time: 30 us; the launch traced here: 29.9 us
  Pallas kernels  29.9 us (100%)
    pallas_call x1, Pallas kernels, body(): pl.pallas_call(functools.partial(panels_kernel, nrow, ncol), out_shape=(p...  25.2 us
    pallas_call x1, Pallas kernels, body(): pl.pallas_call(coupling_kernel, out_shape=jax.ShapeDtypeStruct((npair, mo...  4.73 us

profile of v1, /device:TPU:0, one launch (start us, length us, event | category | flops | bytes accessed | tf_op | source)
XLA Modules:
  0.0 29.9 jit_solution(14709794105295578312)
XLA Ops:
  0.0 25.2 %panels.1 = (bf16[2,12,256,256]{3,2,1,0:T(8,128)(2,1)S(1)}, bf16[2,4,2,256,256]{4,3,2,1,0:T(8,128)(2,1)S(1)}, bf16[8,512,256]{2,1,0:T(8,128)(2,1)S(1)}, s32[8]{0:T(128)S(4)}) custom-call(bf16[12,1024,512]{2,1,0:T(8,128)(2,1)} %phi_hbm.1, bf16[12,256,1024]{2,1,0:T(8,128)(2,1)} %trace_hbm.1, bf16[8,256,256]{2,1,0:T(8,128)(2,1)} %mortar_hbm.1, s32[2,8]{1,0:T(2,128)} %bitcast.1, ...), custom_call_target="tpu_custom_call" | custom-call | tf_op jit(solution)/shard_map/panels/pallas_call | solution.py:192
  25.2 4.7 %coupling.1 = bf16[8,512,512]{2,1,0:T(8,128)(2,1)} custom-call(s32[8]{0:T(128)S(4)} %get-tuple-element.9.route, bf16[2,12,256,256]{3,2,1,0:T(8,128)(2,1)S(1)} %get-tuple-element.10.panels, bf16[2,4,2,256,256]{4,3,2,1,0:T(8,128)(2,1)S(1)} %get-tuple-element.11.arrived, bf16[8,512,256]{2,1,0:T(8,128)(2,1)S(1)} %get-tuple-element.12.left), custom_call_target="tpu_custom_call" | custom-call | tf_op jit(solution)/shard_map/coupling/pallas_call | solution.py:222

commit v2 on v1

v2 whole, which is shorter than its diff:
```python
import functools

import jax
import jax.numpy as jnp
from jax import lax
from jax.experimental import pallas as pl
from jax.experimental.pallas import tpu as pltpu
from jax.sharding import PartitionSpec as P

MESH = pl.DeviceIdType.MESH
ROW_STEPS = (1, 0)
COLUMN_STEPS = (2, 3)
CAP = 2
ROW_BLOCKS = ((0, 128), (128, 128))
COLUMN_BLOCKS = ((0, 256), (256, 256))
PIECES = (((0,), (0,)), ((1,), (0,)), ((0, 1), (1,)))
GROUP = 4


def extent(blocks, chosen):
    return sum(blocks[b][1] for b in chosen)


def panels_kernel(nrow, ncol, *refs):
    refs = list(refs)

    def take(count):
        taken = refs[:count]
        del refs[:count]
        return taken

    phi_hbm, trace_hbm, mortar_hbm, pairs_hbm, counts_hbm = take(5)
    panels, left, route, across = take(4)
    arrived = take(len(PIECES))
    phi = take(len(COLUMN_BLOCKS))
    trace = take(len(ROW_BLOCKS))
    outgoing = take(len(PIECES))
    crossing, mortar, pairs, counts, wanted, asked = take(6)
    phi_sem, trace_sem, small_sem, ask_send, ask_recv = take(5)
    send_sem, recv_sem, cross_send, cross_recv, greeted_sem = take(5)

    owned, iface, modes = panels.shape
    npair = mortar.shape[0]
    row = lax.axis_index("row")
    col = lax.axis_index("col")
    mine = row * ncol + col
    near = [
        (lax.rem(row + nrow - 1, nrow), col),
        (lax.rem(row + 1, nrow), col),
        (row, lax.rem(col + ncol - 1, ncol)),
        (row, lax.rem(col + 1, ncol)),
    ]
    exists = [row > 0, row < nrow - 1, None, None]

    def where_near(d, action):
        if exists[d] is None:
            action()
        else:
            pl.when(exists[d])(action)

    odd = lax.rem(col, 2) == 1
    barrier = pltpu.get_barrier_semaphore()

    def greet(d):
        pl.semaphore_signal(barrier, inc=1, device_id=near[d], device_id_type=MESH)

    for d in ROW_STEPS:
        where_near(d, lambda: greet(d))

    @pl.when(jnp.logical_not(odd))
    def _():
        for d in COLUMN_STEPS:
            greet(d)

    def trace_copy(b, s):
        first, size = ROW_BLOCKS[b]
        return pltpu.make_async_copy(
            trace_hbm.at[s, pl.ds(first, size)], trace[b].at[s], trace_sem.at[b, s]
        )

    def phi_copy(b, s):
        first, size = COLUMN_BLOCKS[b]
        return pltpu.make_async_copy(
            phi_hbm.at[s, :, pl.ds(first, size)], phi[b].at[s], phi_sem.at[b, s]
        )

    pairs_copy = pltpu.make_async_copy(pairs_hbm, pairs, small_sem.at[0])
    counts_copy = pltpu.make_async_copy(counts_hbm, counts, small_sem.at[1])
    mortar_copy = pltpu.make_async_copy(mortar_hbm, mortar, small_sem.at[2])
    pairs_copy.start()
    counts_copy.start()

    loads = []
    for rows, columns in PIECES:
        loads += [(trace_copy, b) for b in rows if (trace_copy, b) not in loads]
        loads += [(phi_copy, b) for b in columns if (phi_copy, b) not in loads]
    for load, b in loads:
        @pl.loop(0, owned)
        def _(s):
            load(b, s).start()

    mortar_copy.start()
    pairs_copy.wait()
    counts_copy.wait()

    base = [(r * ncol + k) * owned for r, k in near]
    taken = [jnp.int32(0)] * 4
    first = [jnp.int32(0)] * 4
    second = [jnp.int32(0)] * 4
    for p in range(npair):
        j = pairs[1, p]
        place = jnp.clip(j - mine * owned, 0, owned - 1)
        for d in range(4):
            local = j - base[d]
            hit = (local >= 0) & (local < owned)
            first[d] = jnp.where(hit & (taken[d] == 0), local, first[d])
            second[d] = jnp.where(hit & (taken[d] == 1), local, second[d])
            slot = owned + CAP * d + jnp.minimum(taken[d], CAP - 1)
            place = jnp.where(hit, slot, place)
            taken[d] = taken[d] + hit.astype(jnp.int32)
        route[p] = place
    for d in range(4):
        wanted[d, 0] = first[d]
        wanted[d, 1] = second[d]

    greeted = exists[0].astype(jnp.int32) + exists[1].astype(jnp.int32)
    pl.semaphore_wait(barrier, greeted + jnp.where(odd, 2, 0))

    @pl.when(odd)
    def _():
        for d in COLUMN_STEPS:
            pl.semaphore_signal(
                greeted_sem, inc=1, device_id=near[d], device_id_type=MESH
            )

    asks = [
        pltpu.make_async_remote_copy(
            src_ref=wanted.at[d],
            dst_ref=asked.at[d ^ 1],
            send_sem=ask_send.at[d],
            recv_sem=ask_recv.at[d ^ 1],
            device_id=near[d],
            device_id_type=MESH,
        )
        for d in range(4)
    ]
    for d in ROW_STEPS:
        where_near(d, asks[d].start)

    def answer(d):
        where_near(d, asks[d ^ 1].wait_recv)

    def product(s, rows, columns):
        maps = jnp.concatenate([trace[b][s] for b in rows], axis=0)
        modes = jnp.concatenate([phi[b][s] for b in columns], axis=1)
        product = jnp.dot(maps, modes, preferred_element_type=jnp.float32)
        return product.astype(panels.dtype)

    waited = set()
    sends = []
    for n, (rows, columns) in enumerate(PIECES):
        fresh = [(trace_copy, b) for b in rows] + [(phi_copy, b) for b in columns]
        fresh = [item for item in fresh if item not in waited]
        waited.update(fresh)

        @pl.loop(0, owned)
        def _(s):
            for load, b in fresh:
                load(b, s).wait()

        for d in ROW_STEPS:
            if n == 0:
                answer(d)
            send = pltpu.make_async_remote_copy(
                src_ref=outgoing[n].at[d],
                dst_ref=arrived[n].at[d ^ 1],
                send_sem=send_sem.at[n, d],
                recv_sem=recv_sem.at[n, d ^ 1],
                device_id=near[d],
                device_id_type=MESH,
            )

            def project():
                for k in range(CAP):
                    outgoing[n][d, k] = product(asked[d, k], rows, columns)
                send.start()

            where_near(d, project)
            sends.append((d, send))
        if n == 0:
            @pl.when(jnp.logical_not(odd))
            def _():
                pl.semaphore_wait(greeted_sem, 2)

            for d in COLUMN_STEPS:
                asks[d].start()

    all_rows = tuple(range(len(ROW_BLOCKS)))
    all_columns = tuple(range(len(COLUMN_BLOCKS)))
    for d in COLUMN_STEPS:
        answer(d)
        for k in range(CAP):
            crossing[d - 2, k] = product(asked[d, k], all_rows, all_columns)
        send = pltpu.make_async_remote_copy(
            src_ref=crossing.at[d - 2],
            dst_ref=across.at[(d ^ 1) - 2],
            send_sem=cross_send.at[d - 2],
            recv_sem=cross_recv.at[(d ^ 1) - 2],
            device_id=near[d],
            device_id_type=MESH,
        )
        send.start()
        sends.append((d, send))

    @pl.loop(0, owned // GROUP)
    def _(g):
        for u in range(GROUP):
            panels[g * GROUP + u] = product(g * GROUP + u, all_rows, all_columns)

    mortar_copy.wait()
    row_ids = lax.broadcasted_iota(jnp.int32, (iface, iface), 0)
    column_ids = lax.broadcasted_iota(jnp.int32, (iface, iface), 1)

    @pl.loop(0, npair)
    def _(p):
        own = jnp.clip(pairs[0, p] - mine * owned, 0, owned - 1)
        count = counts[p]
        keep = (row_ids < count) & (column_ids < count)
        masked = jnp.where(keep, mortar[p].astype(jnp.float32), 0.0).astype(mortar.dtype)
        left[p] = lax.dot_general(
            panels[own],
            masked,
            (((0,), (0,)), ((), ())),
            preferred_element_type=jnp.float32,
        ).astype(left.dtype)

    for d in range(4):
        where_near(d, asks[d].wait_send)
    along_column = [item for item in sends if item[0] in COLUMN_STEPS]
    along_row = [item for item in sends if item[0] in ROW_STEPS]
    for d, send in along_column + along_row:
        where_near(d, send.wait_send)
    for d, send in along_column + along_row:
        where_near(d ^ 1, send.wait_recv)


def coupling_kernel(route, panels, left, across, *refs):
    arrived = refs[: len(PIECES)]
    coupling_hbm, coupling, out_sem = refs[len(PIECES) :]
    owned = panels.shape[0]
    copies = []
    for p in range(left.shape[0]):
        place = route[p]
        inside = jnp.minimum(place, owned - 1)
        slot = jnp.maximum(place - owned, 0)
        step = slot // CAP
        along_row = jnp.minimum(step, 1)
        along_column = jnp.maximum(step - 2, 0)
        k = slot % CAP
        columns = []
        for c in range(len(COLUMN_BLOCKS)):
            parts = [arrived[n][along_row, k] for n in range(len(PIECES)) if PIECES[n][1] == (c,)]
            columns.append(jnp.concatenate(parts, axis=0))
        partner = jnp.concatenate(columns, axis=1)
        partner = lax.select(step >= 2, across[along_column, k], partner)
        partner = lax.select(place < owned, panels[inside], partner)
        coupling[p] = jnp.dot(
            left[p], partner, preferred_element_type=jnp.float32
        ).astype(coupling.dtype)
        copy = pltpu.make_async_copy(coupling.at[p], coupling_hbm.at[p], out_sem.at[p])
        copy.start()
        copies.append(copy)
    for copy in copies:
        copy.wait()


def body(nrow, ncol, phi_modes, trace_maps, mortar, pair_list, iface_counts):
    owned, boundary, modes = phi_modes.shape
    npair, iface, _ = mortar.shape
    dtype = phi_modes.dtype
    hbm = pl.BlockSpec(memory_space=pltpu.HBM)
    smem = pl.BlockSpec(memory_space=pltpu.SMEM)
    vmem = pl.BlockSpec(memory_space=pltpu.VMEM)
    dma = pltpu.SemaphoreType.DMA
    count = len(PIECES)
    pieces = [
        pltpu.VMEM((2, CAP, extent(ROW_BLOCKS, r), extent(COLUMN_BLOCKS, c)), dtype)
        for r, c in PIECES
    ]
    across = pltpu.VMEM((2, CAP, iface, modes), dtype)
    panels, left, route, across_in, *arrived = pl.pallas_call(
        functools.partial(panels_kernel, nrow, ncol),
        out_shape=(
            pltpu.VMEM((owned, iface, modes), dtype),
            pltpu.VMEM((npair, modes, iface), dtype),
            pltpu.SMEM((npair,), jnp.int32),
            across,
            *pieces,
        ),
        in_specs=[hbm] * 5,
        out_specs=(vmem, vmem, smem, vmem, *[vmem] * count),
        scratch_shapes=[
            *[pltpu.VMEM((owned, boundary, size), dtype) for _, size in COLUMN_BLOCKS],
            *[pltpu.VMEM((owned, size, boundary), dtype) for _, size in ROW_BLOCKS],
            *pieces,
            across,
            pltpu.VMEM((npair, iface, iface), dtype),
            pltpu.SMEM((2, npair), jnp.int32),
            pltpu.SMEM((npair,), jnp.int32),
            pltpu.SMEM((4, 128), jnp.int32),
            pltpu.SMEM((4, 128), jnp.int32),
            dma((len(COLUMN_BLOCKS), owned)),
            dma((len(ROW_BLOCKS), owned)),
            dma((3,)),
            dma((4,)),
            dma((4,)),
            dma((count, 2)),
            dma((count, 2)),
            dma((2,)),
            dma((2,)),
            pltpu.SemaphoreType.REGULAR,
        ],
        compiler_params=pltpu.CompilerParams(
            collective_id=0, has_side_effects=True, vmem_limit_bytes=48 * 2**20
        ),
        name="panels",
    )(phi_modes, trace_maps, mortar, pair_list.T, iface_counts)
    return pl.pallas_call(
        coupling_kernel,
        out_shape=jax.ShapeDtypeStruct((npair, modes, modes), dtype),
        in_specs=[smem, vmem, vmem, vmem, *[vmem] * count],
        out_specs=hbm,
        scratch_shapes=[pltpu.VMEM((npair, modes, modes), dtype), dma((npair,))],
        compiler_params=pltpu.CompilerParams(vmem_limit_bytes=32 * 2**20),
        name="coupling",
    )(route, panels, left, across_in, *arrived)


def solution(mesh):
    return jax.shard_map(
        functools.partial(body, mesh.shape["row"], mesh.shape["col"]),
        mesh=mesh,
        in_specs=(
            P(("row", "col"), None, None),
            P(("row", "col"), None, None),
            P(("row", "col"), None, None),
            P(("row", "col"), None),
            P(("row", "col")),
        ),
        out_specs=P(("row", "col"), None, None),
        check_vma=False,
    )
```

time: 30 us -> 23.8 us (0.79)
  the two profiles are of different devices: /device:TPU:0 before, /device:TPU:22 now
where the time goes in v2:
time: 23.8 us; the launch traced here: 23.7 us
  Pallas kernels  23.7 us (100%)
    pallas_call x1, Pallas kernels, body(): pl.pallas_call(functools.partial(panels_kernel, nrow, ncol), out_shape=(p...  21.3 us
    pallas_call x1, Pallas kernels, body(): pl.pallas_call(coupling_kernel, out_shape=jax.ShapeDtypeStruct((npair, mo...  2.4 us

profile of v2, /device:TPU:22, one launch (start us, length us, event | category | flops | bytes accessed | tf_op | source)
XLA Modules:
  0.0 23.7 jit_solution(8620243653995894160)
XLA Ops:
  0.0 21.3 %panels.1 = (bf16[12,256,512]{2,1,0:T(8,128)(2,1)S(1)}, bf16[8,512,256]{2,1,0:T(8,128)(2,1)S(1)}, s32[8]{0:T(128)S(4)}, bf16[2,2,256,512]{3,2,1,0:T(8,128)(2,1)S...) custom-call(bf16[12,1024,512]{2,1,0:T(8,128)(2,1)} %refs_0_.1, ...), custom_call_target="tpu_custom_call" | custom-call | tf_op jit(solution)/shard_map/panels/pallas_call | solution.py:291
  21.3 2.4 %coupling.1 = bf16[8,512,512]{2,1,0:T(8,128)(2,1)} custom-call(s32[8]{0:T(128)S(4)} %get-tuple-element.12.route, bf16[12,256,512]{2,1,0:T(8,128)(2,1)S(1)} %get-tuple-element.13.panels, bf16[8,512,256]{2,1,0:T(8,128)(2,1)S(1)} %get-tuple-element.14.left, bf16[2,2,256,512]{3,2,1,0:T(8,128)(2,1)S(1)} %get-tuple-element.15.across, ...), custom_call_target="tpu_custom_call" | custom-call | tf_op jit(solution)/shard_map/coupling/pallas_call | solution.py:328

commit v3 on v2

--- a/solution.py
+++ b/solution.py
@@ -14,6 +14,8 @@
 ROW_BLOCKS = ((0, 128), (128, 128))
 COLUMN_BLOCKS = ((0, 256), (256, 256))
 PIECES = (((0,), (0,)), ((1,), (0,)), ((0, 1), (1,)))
+PLANE = 4
+PASSED = (((0,), 64, (0, 1)), ((0,), 64, (0, 1)), ((7, 0), 64, (0,)))
 GROUP = 4
 
 
@@ -38,6 +40,8 @@
     crossing, mortar, pairs, counts, wanted, asked = take(6)
     phi_sem, trace_sem, small_sem, ask_send, ask_recv = take(5)
     send_sem, recv_sem, cross_send, cross_recv, greeted_sem = take(5)
+    passing = take(len(PASSED))
+    passing_recv, passing_send = take(2)
 
     owned, iface, modes = panels.shape
     npair = mortar.shape[0]
@@ -58,7 +62,17 @@
         else:
             pl.when(exists[d])(action)
 
+    ways = [
+        (PLANE * x + PLANE - 1, *by, PLANE * (x + 1)) for x, (by, _, _) in enumerate(PASSED)
+    ]
+
     odd = lax.rem(col, 2) == 1
+
+    def is_at(x, place):
+        if len(PASSED[x][2]) == 2:
+            return row == place
+        return (row == place) & (lax.rem(col, 2) == PASSED[x][2][0])
+
     barrier = pltpu.get_barrier_semaphore()
 
     def greet(d):
@@ -66,6 +80,15 @@
 
     for d in ROW_STEPS:
         where_near(d, lambda: greet(d))
+
+    def greet_row(other):
+        pl.semaphore_signal(
+            barrier, inc=1, device_id=(jnp.int32(other), col), device_id_type=MESH
+        )
+
+    for x, way in enumerate(ways):
+        for source, target in zip(way, way[1:]):
+            pl.when(is_at(x, target))(lambda: greet_row(source))
 
     @pl.when(jnp.logical_not(odd))
     def _():
@@ -124,6 +147,9 @@
         wanted[d, 1] = second[d]
 
     greeted = exists[0].astype(jnp.int32) + exists[1].astype(jnp.int32)
+    for x, way in enumerate(ways):
+        for source in way[:-1]:
+            greeted = greeted + is_at(x, source).astype(jnp.int32)
     pl.semaphore_wait(barrier, greeted + jnp.where(odd, 2, 0))
 
     @pl.when(odd)
@@ -156,6 +182,62 @@
         product = jnp.dot(maps, modes, preferred_element_type=jnp.float32)
         return product.astype(panels.dtype)
 
+    def start_split(send):
+        direct = row < nrow
+        for x, way in enumerate(ways):
+            size = PASSED[x][1]
+            direct = direct & jnp.logical_not(is_at(x, way[0]))
+
+            @pl.when(is_at(x, way[0]))
+            def _():
+                pltpu.make_async_remote_copy(
+                    src_ref=outgoing[0].at[1, :, pl.ds(0, size)],
+                    dst_ref=passing[x],
+                    send_sem=send_sem.at[0, 1],
+                    recv_sem=passing_recv.at[x],
+                    device_id=(jnp.int32(way[1]), col),
+                    device_id_type=MESH,
+                ).start()
+                rest = pl.ds(size, outgoing[0].shape[2] - size)
+                pltpu.make_async_remote_copy(
+                    src_ref=outgoing[0].at[1, :, rest],
+                    dst_ref=arrived[0].at[0, :, rest],
+                    send_sem=send_sem.at[0, 1],
+                    recv_sem=recv_sem.at[0, 0],
+                    device_id=near[1],
+                    device_id_type=MESH,
+                ).start()
+
+        pl.when(direct)(send.start)
+
+    def passed_on(x, hop):
+        final = hop == len(ways[x]) - 2
+        target = arrived[0].at[0, :, pl.ds(0, PASSED[x][1])]
+        return pltpu.make_async_remote_copy(
+            src_ref=passing[x],
+            dst_ref=target if final else passing[x],
+            send_sem=passing_send.at[x],
+            recv_sem=recv_sem.at[0, 0] if final else passing_recv.at[x],
+            device_id=(jnp.int32(ways[x][hop + 1]), col),
+            device_id_type=MESH,
+        )
+
+    def pass_on(x, hop):
+        way = ways[x]
+
+        @pl.when(is_at(x, way[hop]))
+        def _():
+            pltpu.make_async_remote_copy(
+                src_ref=passing[x],
+                dst_ref=passing[x],
+                send_sem=passing_send.at[x],
+                recv_sem=passing_recv.at[x],
+                device_id=(jnp.int32(way[hop + 1]), col),
+                device_id_type=MESH,
+            ).wait_recv()
+            passed_on(x, hop).start()
+
+    held = []
     waited = set()
     sends = []
     for n, (rows, columns) in enumerate(PIECES):
@@ -183,9 +265,18 @@
             def project():
                 for k in range(CAP):
                     outgoing[n][d, k] = product(asked[d, k], rows, columns)
-                send.start()
+
+            def start(n=n, d=d, send=send):
+                if d == 1 and n == 0:
+                    start_split(send)
+                else:
+                    send.start()
 
             where_near(d, project)
+            if n == len(PIECES) - 1:
+                held.append((d, start))
+            else:
+                where_near(d, start)
             sends.append((d, send))
         if n == 0:
             @pl.when(jnp.logical_not(odd))
@@ -194,6 +285,10 @@
 
             for d in COLUMN_STEPS:
                 asks[d].start()
+
+    pass_on(2, 1)
+    for d, start in held:
+        where_near(d, start)
 
     all_rows = tuple(range(len(ROW_BLOCKS)))
     all_columns = tuple(range(len(COLUMN_BLOCKS)))
@@ -217,6 +312,9 @@
         for u in range(GROUP):
             panels[g * GROUP + u] = product(g * GROUP + u, all_rows, all_columns)
 
+    pass_on(0, 1)
+    pass_on(1, 1)
+    pass_on(2, 2)
     mortar_copy.wait()
     row_ids = lax.broadcasted_iota(jnp.int32, (iface, iface), 0)
     column_ids = lax.broadcasted_iota(jnp.int32, (iface, iface), 1)
@@ -236,6 +334,9 @@
 
     for d in range(4):
         where_near(d, asks[d].wait_send)
+    for x, way in enumerate(ways):
+        for hop in range(1, len(way) - 1):
+            pl.when(is_at(x, way[hop]))(passed_on(x, hop).wait_send)
     along_column = [item for item in sends if item[0] in COLUMN_STEPS]
     along_row = [item for item in sends if item[0] in ROW_STEPS]
     for d, send in along_column + along_row:
@@ -319,6 +420,9 @@
             dma((2,)),
             dma((2,)),
             pltpu.SemaphoreType.REGULAR,
+            *[pltpu.VMEM((CAP, size, pieces[0].shape[3]), dtype) for _, size, _ in PASSED],
+            dma((len(PASSED),)),
+            dma((len(PASSED),)),
         ],
         compiler_params=pltpu.CompilerParams(
             collective_id=0, has_side_effects=True, vmem_limit_bytes=48 * 2**20

time: 23.8 us -> 23.3 us (0.979)
  Pallas kernels: 23.7 us -> 23.1 us
    pallas_call x1, Pallas kernels: 21.3 us -> 20.8 us  [body(): pl.pallas_call(functools.partial(panels_kernel, nrow, ncol), out_shape=(p...]
where the time goes in v3:
time: 23.3 us; the launch traced here: 23.2 us
  Pallas kernels  23.1 us (99%)
    pallas_call x1, Pallas kernels, body(): pl.pallas_call(functools.partial(panels_kernel, nrow, ncol), out_shape=(p...  20.8 us
    pallas_call x1, Pallas kernels, body(): pl.pallas_call(coupling_kernel, out_shape=jax.ShapeDtypeStruct((npair, mo...  2.4 us

profile of v3, /device:TPU:22, one launch (start us, length us, event | category | flops | bytes accessed | tf_op | source)
XLA Modules:
  0.0 23.2 jit_solution(8999632819875067298)
XLA Ops:
  0.0 20.8 %panels.1 = (bf16[12,256,512]{2,1,0:T(8,128)(2,1)S(1)}, bf16[8,512,256]{2,1,0:T(8,128)(2,1)S(1)}, s32[8]{0:T(128)S(4)}, bf16[2,2,256,512]{3,2,1,0:T(8,128)(2,1)S...) custom-call(bf16[12,1024,512]{2,1,0:T(8,128)(2,1)} %refs_0_.1, ...), custom_call_target="tpu_custom_call" | custom-call | tf_op jit(solution)/shard_map/panels/pallas_call | solution.py:392
  20.8 2.4 %coupling.1 = bf16[8,512,512]{2,1,0:T(8,128)(2,1)} custom-call(s32[8]{0:T(128)S(4)} %get-tuple-element.12.route, bf16[12,256,512]{2,1,0:T(8,128)(2,1)S(1)} %get-tuple-element.13.panels, bf16[8,512,256]{2,1,0:T(8,128)(2,1)S(1)} %get-tuple-element.14.left, bf16[2,2,256,512]{3,2,1,0:T(8,128)(2,1)S(1)} %get-tuple-element.15.across, ...), custom_call_target="tpu_custom_call" | custom-call | tf_op jit(solution)/shard_map/coupling/pallas_call | solution.py:432

commit v4 on v3

--- a/solution.py
+++ b/solution.py
@@ -16,6 +16,7 @@
 PIECES = (((0,), (0,)), ((1,), (0,)), ((0, 1), (1,)))
 PLANE = 4
 PASSED = (((0,), 64, (0, 1)), ((0,), 64, (0, 1)), ((7, 0), 64, (0,)))
+FIRST_PARTS = 2
 GROUP = 4
 
 
@@ -32,12 +33,11 @@
         return taken
 
     phi_hbm, trace_hbm, mortar_hbm, pairs_hbm, counts_hbm = take(5)
-    panels, left, route, across = take(4)
-    arrived = take(len(PIECES))
+    table, left, route = take(3)
     phi = take(len(COLUMN_BLOCKS))
     trace = take(len(ROW_BLOCKS))
     outgoing = take(len(PIECES))
-    crossing, mortar, pairs, counts, wanted, asked = take(6)
+    crossing, panels, mortar, pairs, counts, wanted, asked = take(7)
     phi_sem, trace_sem, small_sem, ask_send, ask_recv = take(5)
     send_sem, recv_sem, cross_send, cross_recv, greeted_sem = take(5)
     passing = take(len(PASSED))
@@ -176,6 +176,18 @@
     def answer(d):
         where_near(d, asks[d ^ 1].wait_recv)
 
+    def arriving(d, rows, columns):
+        return table.at[pl.ds(owned + CAP * d, CAP), pl.ds(*rows), pl.ds(*columns)]
+
+    def piece_arriving(n, d, first=0, size=None):
+        rows, columns = PIECES[n]
+        size = extent(ROW_BLOCKS, rows) if size is None else size
+        return arriving(
+            d,
+            (ROW_BLOCKS[rows[0]][0] + first, size),
+            (COLUMN_BLOCKS[columns[0]][0], extent(COLUMN_BLOCKS, columns)),
+        )
+
     def product(s, rows, columns):
         maps = jnp.concatenate([trace[b][s] for b in rows], axis=0)
         modes = jnp.concatenate([phi[b][s] for b in columns], axis=1)
@@ -198,10 +210,10 @@
                     device_id=(jnp.int32(way[1]), col),
                     device_id_type=MESH,
                 ).start()
-                rest = pl.ds(size, outgoing[0].shape[2] - size)
+                kept = outgoing[0].shape[2] - size
                 pltpu.make_async_remote_copy(
-                    src_ref=outgoing[0].at[1, :, rest],
-                    dst_ref=arrived[0].at[0, :, rest],
+                    src_ref=outgoing[0].at[1, :, pl.ds(size, kept)],
+                    dst_ref=piece_arriving(0, 0, size, kept),
                     send_sem=send_sem.at[0, 1],
                     recv_sem=recv_sem.at[0, 0],
                     device_id=near[1],
@@ -212,7 +224,7 @@
 
     def passed_on(x, hop):
         final = hop == len(ways[x]) - 2
-        target = arrived[0].at[0, :, pl.ds(0, PASSED[x][1])]
+        target = piece_arriving(0, 0, 0, PASSED[x][1])
         return pltpu.make_async_remote_copy(
             src_ref=passing[x],
             dst_ref=target if final else passing[x],
@@ -237,7 +249,33 @@
             ).wait_recv()
             passed_on(x, hop).start()
 
-    held = []
+    def piece_send(n, d):
+        return pltpu.make_async_remote_copy(
+            src_ref=outgoing[n].at[d],
+            dst_ref=piece_arriving(n, d ^ 1),
+            send_sem=send_sem.at[n, d],
+            recv_sem=recv_sem.at[n, d ^ 1],
+            device_id=near[d],
+            device_id_type=MESH,
+        )
+
+    def project(n, d):
+        for k in range(CAP):
+            outgoing[n][d, k] = product(asked[d, k], *PIECES[n])
+
+    def start(n, d):
+        if d == 1 and n == 0:
+            start_split(piece_send(n, d))
+        else:
+            piece_send(n, d).start()
+
+    def serve(n, order):
+        for d in order:
+            if n == 0:
+                answer(d)
+            where_near(d, lambda: project(n, d))
+            where_near(d, lambda: start(n, d))
+
     waited = set()
     sends = []
     for n, (rows, columns) in enumerate(PIECES):
@@ -250,34 +288,24 @@
             for load, b in fresh:
                 load(b, s).wait()
 
-        for d in ROW_STEPS:
-            if n == 0:
-                answer(d)
-            send = pltpu.make_async_remote_copy(
-                src_ref=outgoing[n].at[d],
-                dst_ref=arrived[n].at[d ^ 1],
-                send_sem=send_sem.at[n, d],
-                recv_sem=recv_sem.at[n, d ^ 1],
-                device_id=near[d],
-                device_id_type=MESH,
-            )
-
-            def project():
-                for k in range(CAP):
-                    outgoing[n][d, k] = product(asked[d, k], rows, columns)
-
-            def start(n=n, d=d, send=send):
-                if d == 1 and n == 0:
-                    start_split(send)
-                else:
-                    send.start()
-
-            where_near(d, project)
-            if n == len(PIECES) - 1:
-                held.append((d, start))
-            else:
-                where_near(d, start)
-            sends.append((d, send))
+        if n < len(PIECES) - 1:
+            serve(n, ROW_STEPS)
+        else:
+            midway = is_at(2, ways[2][1])
+
+            @pl.when(jnp.logical_not(midway))
+            def _():
+                serve(n, ROW_STEPS)
+
+            @pl.when(midway)
+            def _():
+                for d in ROW_STEPS:
+                    where_near(d, lambda: project(n, d))
+                pass_on(2, 1)
+                for d in ROW_STEPS:
+                    where_near(d, lambda: start(n, d))
+
+        sends += [(d, piece_send(n, d)) for d in ROW_STEPS]
         if n == 0:
             @pl.when(jnp.logical_not(odd))
             def _():
@@ -285,10 +313,6 @@
 
             for d in COLUMN_STEPS:
                 asks[d].start()
-
-    pass_on(2, 1)
-    for d, start in held:
-        where_near(d, start)
 
     all_rows = tuple(range(len(ROW_BLOCKS)))
     all_columns = tuple(range(len(COLUMN_BLOCKS)))
@@ -298,7 +322,7 @@
             crossing[d - 2, k] = product(asked[d, k], all_rows, all_columns)
         send = pltpu.make_async_remote_copy(
             src_ref=crossing.at[d - 2],
-            dst_ref=across.at[(d ^ 1) - 2],
+            dst_ref=arriving(d ^ 1, (0, iface), (0, modes)),
             send_sem=cross_send.at[d - 2],
             recv_sem=cross_recv.at[(d ^ 1) - 2],
             device_id=near[d],
@@ -310,7 +334,9 @@
     @pl.loop(0, owned // GROUP)
     def _(g):
         for u in range(GROUP):
-            panels[g * GROUP + u] = product(g * GROUP + u, all_rows, all_columns)
+            panel = product(g * GROUP + u, all_rows, all_columns)
+            panels[g * GROUP + u] = panel
+            table[g * GROUP + u] = panel
 
     pass_on(0, 1)
     pass_on(1, 1)
@@ -345,32 +371,23 @@
         where_near(d ^ 1, send.wait_recv)
 
 
-def coupling_kernel(route, panels, left, across, *refs):
-    arrived = refs[: len(PIECES)]
-    coupling_hbm, coupling, out_sem = refs[len(PIECES) :]
-    owned = panels.shape[0]
+def coupling_kernel(route, table, left, coupling_hbm, coupling, out_sem):
+    npair, modes, _ = left.shape
     copies = []
-    for p in range(left.shape[0]):
-        place = route[p]
-        inside = jnp.minimum(place, owned - 1)
-        slot = jnp.maximum(place - owned, 0)
-        step = slot // CAP
-        along_row = jnp.minimum(step, 1)
-        along_column = jnp.maximum(step - 2, 0)
-        k = slot % CAP
-        columns = []
-        for c in range(len(COLUMN_BLOCKS)):
-            parts = [arrived[n][along_row, k] for n in range(len(PIECES)) if PIECES[n][1] == (c,)]
-            columns.append(jnp.concatenate(parts, axis=0))
-        partner = jnp.concatenate(columns, axis=1)
-        partner = lax.select(step >= 2, across[along_column, k], partner)
-        partner = lax.select(place < owned, panels[inside], partner)
-        coupling[p] = jnp.dot(
-            left[p], partner, preferred_element_type=jnp.float32
-        ).astype(coupling.dtype)
-        copy = pltpu.make_async_copy(coupling.at[p], coupling_hbm.at[p], out_sem.at[p])
-        copy.start()
-        copies.append(copy)
+    for p in range(npair):
+        partner = table[route[p]]
+        parts = FIRST_PARTS if p == 0 else 1
+        rows = modes // parts
+        for part in range(parts):
+            block = (p, pl.ds(part * rows, rows))
+            coupling[block] = jnp.dot(
+                left[block], partner, preferred_element_type=jnp.float32
+            ).astype(coupling.dtype)
+            copy = pltpu.make_async_copy(
+                coupling.at[block], coupling_hbm.at[block], out_sem.at[len(copies)]
+            )
+            copy.start()
+            copies.append(copy)
     for copy in copies:
         copy.wait()
 
@@ -388,23 +405,21 @@
         pltpu.VMEM((2, CAP, extent(ROW_BLOCKS, r), extent(COLUMN_BLOCKS, c)), dtype)
         for r, c in PIECES
     ]
-    across = pltpu.VMEM((2, CAP, iface, modes), dtype)
-    panels, left, route, across_in, *arrived = pl.pallas_call(
+    table, left, route = pl.pallas_call(
         functools.partial(panels_kernel, nrow, ncol),
         out_shape=(
-            pltpu.VMEM((owned, iface, modes), dtype),
+            pltpu.VMEM((owned + 4 * CAP, iface, modes), dtype),
             pltpu.VMEM((npair, modes, iface), dtype),
             pltpu.SMEM((npair,), jnp.int32),
-            across,
-            *pieces,
         ),
         in_specs=[hbm] * 5,
-        out_specs=(vmem, vmem, smem, vmem, *[vmem] * count),
+        out_specs=(vmem, vmem, smem),
         scratch_shapes=[
             *[pltpu.VMEM((owned, boundary, size), dtype) for _, size in COLUMN_BLOCKS],
             *[pltpu.VMEM((owned, size, boundary), dtype) for _, size in ROW_BLOCKS],
             *pieces,
-            across,
+            pltpu.VMEM((2, CAP, iface, modes), dtype),
+            pltpu.VMEM((owned, iface, modes), dtype),
             pltpu.VMEM((npair, iface, iface), dtype),
             pltpu.SMEM((2, npair), jnp.int32),
             pltpu.SMEM((npair,), jnp.int32),
@@ -432,12 +447,12 @@
     return pl.pallas_call(
         coupling_kernel,
         out_shape=jax.ShapeDtypeStruct((npair, modes, modes), dtype),
-        in_specs=[smem, vmem, vmem, vmem, *[vmem] * count],
+        in_specs=[smem, vmem, vmem],
         out_specs=hbm,
-        scratch_shapes=[pltpu.VMEM((npair, modes, modes), dtype), dma((npair,))],
+        scratch_shapes=[pltpu.VMEM((npair, modes, modes), dtype), dma((npair + FIRST_PARTS - 1,))],
         compiler_params=pltpu.CompilerParams(vmem_limit_bytes=32 * 2**20),
         name="coupling",
-    )(route, panels, left, across_in, *arrived)
+    )(route, table, left)
 
 
 def solution(mesh):

time: 23.3 us -> 23.2 us (level)
  no operation moved by 1% of the time
where the time goes in v4:
time: 23.2 us; the launch traced here: 23.1 us
  Pallas kernels  23.1 us (100%)
    pallas_call x1, Pallas kernels, body(): pl.pallas_call(functools.partial(panels_kernel, nrow, ncol), out_shape=(p...  20.8 us
    pallas_call x1, Pallas kernels, body(): pl.pallas_call(coupling_kernel, out_shape=jax.ShapeDtypeStruct((npair, mo...  2.35 us

profile of v4, /device:TPU:22, one launch (start us, length us, event | category | flops | bytes accessed | tf_op | source)
XLA Modules:
  0.0 23.1 jit_solution(8639982230118192801)
XLA Ops:
  0.0 20.8 %panels.1 = (bf16[20,256,512]{2,1,0:T(8,128)(2,1)S(1)}, bf16[8,512,256]{2,1,0:T(8,128)(2,1)S(1)}, s32[8]{0:T(128)S(4)}) custom-call(bf16[12,1024,512]{2,1,0:T(8,128)(2,1)} %refs_0_.1, bf16[12,256,1024]{2,1,0:T(8,128)(2,1)} %refs_1_.1, bf16[8,256,256]{2,1,0:T(8,128)(2,1)} %refs_2_.1, s32[2,8]{1,0:T(2,128)} %bitcast.1, s32[8]{0:T(128)} %refs_4_.1), custom_call_target="tpu_custom_call" | custom-call | tf_op jit(solution)/shard_map/panels/pallas_call | solution.py:408
  20.8 2.3 %coupling.1 = bf16[8,512,512]{2,1,0:T(8,128)(2,1)} custom-call(s32[8]{0:T(128)S(4)} %get-tuple-element.8.route, bf16[20,256,512]{2,1,0:T(8,128)(2,1)S(1)} %get-tuple-element.9.table, bf16[8,512,256]{2,1,0:T(8,128)(2,1)S(1)} %get-tuple-element.10.left), custom_call_target="tpu_custom_call" | custom-call | tf_op jit(solution)/shard_map/coupling/pallas_call | solution.py:447

commit v5 on v4

--- a/solution.py
+++ b/solution.py
@@ -15,7 +15,7 @@
 COLUMN_BLOCKS = ((0, 256), (256, 256))
 PIECES = (((0,), (0,)), ((1,), (0,)), ((0, 1), (1,)))
 PLANE = 4
-PASSED = (((0,), 64, (0, 1)), ((0,), 64, (0, 1)), ((7, 0), 64, (0,)))
+PASSED = (((0,), 96, (0, 1)), ((0,), 96, (0, 1)), ((7, 0), 64, (0,)))
 FIRST_PARTS = 2
 GROUP = 4
 
@@ -376,7 +376,7 @@
     copies = []
     for p in range(npair):
         partner = table[route[p]]
-        parts = FIRST_PARTS if p == 0 else 1
+        parts = FIRST_PARTS
         rows = modes // parts
         for part in range(parts):
             block = (p, pl.ds(part * rows, rows))
@@ -449,7 +449,7 @@
         out_shape=jax.ShapeDtypeStruct((npair, modes, modes), dtype),
         in_specs=[smem, vmem, vmem],
         out_specs=hbm,
-        scratch_shapes=[pltpu.VMEM((npair, modes, modes), dtype), dma((npair + FIRST_PARTS - 1,))],
+        scratch_shapes=[pltpu.VMEM((npair, modes, modes), dtype), dma((npair * FIRST_PARTS,))],
         compiler_params=pltpu.CompilerParams(vmem_limit_bytes=32 * 2**20),
         name="coupling",
     )(route, table, left)

time: 23.2 us -> 23.2 us (level)
  no operation moved by 1% of the time
where the time goes in v5:
time: 23.2 us; the launch traced here: 23.1 us
  Pallas kernels  23.1 us (100%)
    pallas_call x1, Pallas kernels, body(): pl.pallas_call(functools.partial(panels_kernel, nrow, ncol), out_shape=(p...  20.8 us
    pallas_call x1, Pallas kernels, body(): pl.pallas_call(coupling_kernel, out_shape=jax.ShapeDtypeStruct((npair, mo...  2.37 us

profile of v5, /device:TPU:22, one launch (start us, length us, event | category | flops | bytes accessed | tf_op | source)
XLA Modules:
  0.0 23.1 jit_solution(6202271173113495899)
XLA Ops:
  0.0 20.8 %panels.1 = (bf16[20,256,512]{2,1,0:T(8,128)(2,1)S(1)}, bf16[8,512,256]{2,1,0:T(8,128)(2,1)S(1)}, s32[8]{0:T(128)S(4)}) custom-call(bf16[12,1024,512]{2,1,0:T(8,128)(2,1)} %refs_0_.1, bf16[12,256,1024]{2,1,0:T(8,128)(2,1)} %refs_1_.1, bf16[8,256,256]{2,1,0:T(8,128)(2,1)} %refs_2_.1, s32[2,8]{1,0:T(2,128)} %bitcast.1, s32[8]{0:T(128)} %refs_4_.1), custom_call_target="tpu_custom_call" | custom-call | tf_op jit(solution)/shard_map/panels/pallas_call | solution.py:408
  20.8 2.4 %coupling.1 = bf16[8,512,512]{2,1,0:T(8,128)(2,1)} custom-call(s32[8]{0:T(128)S(4)} %get-tuple-element.8.route, bf16[20,256,512]{2,1,0:T(8,128)(2,1)S(1)} %get-tuple-element.9.table, bf16[8,512,256]{2,1,0:T(8,128)(2,1)S(1)} %get-tuple-element.10.left), custom_call_target="tpu_custom_call" | custom-call | tf_op jit(solution)/shard_map/coupling/pallas_call | solution.py:447
